TPU v7x, 256 devices: a whole 4x4x8 slice. The times are simulated.
256 devices in a mesh: dp: 32 (over y, z_hi, core), tensor: 8 (over x, z_lo).
Axes of the slice: x: 4, y: 4, z: 8 (z_hi: 4, z_lo: 2; z = z_hi * 2 + z_lo), core: 2. Of those that a mesh axis runs over, the one named last changes fastest.
Arguments:
- prefix_cache: bfloat16 [32, 2048, 2048], P('dp', None, 'tensor'), may hold values from -6 to 6
- prefix_len: int32 [32], P('dp'), may hold values from 1 to 2048, 40960 in all
- decode_q: bfloat16 [512, 4096], P('dp', 'tensor'), may hold values from -130 to 130
- sample_kv: bfloat16 [512, 2048], P('dp', 'tensor'), may hold values from -6 to 6
- sample_count: int32 [32], P('dp'), may hold values from 1 to 16, 384 in all
- sectioned_pages: bfloat16 [768, 128, 2048], P('dp', None, 'tensor'), may hold values from -6 to 6
- page_owner: int32 [768, 1], P('dp'), may hold values from 0 to 31; in each aligned block of 24 rows (0 to 23, 24 to 47, ...) at most 2 rows name the same one
- prefill_q: bfloat16 [65536, 4096], P('dp', 'tensor'), may hold values from -130 to 130
- prefill_kv: bfloat16 [65536, 2048], P('dp', 'tensor'), may hold values from -6 to 6
- span_len: int32 [32], P('dp'), may hold values from 1 to 2048, 40960 in all
- out_weight: bfloat16 [4096, 4096], P('tensor'), may hold values from -0.09375 to 0.09375
Outputs:
- decode_out: bfloat16 [512, 4096], P('dp', 'tensor')
- prefill_out: bfloat16 [65536, 4096], P('dp', 'tensor')
Inputs may be any that keep to these rules, and one draw needn't show every extreme that they name: `page_owner`: in the 24 sectioned pages of one group no prompt is named more than 2 times.
All inputs are finite; a program needn't handle non-finite values. No bound on the sum of `prefix_len` or of `sample_count` or of `span_len` on one device may be relied on, other than what follows from the above.
Results may differ from a plain program's by a relative error of at most 0.019.
Values may be sent and summed in bfloat16 or wider, within the bound.
A program may use at most 64 MiB of HBM per device.

v0:
```python
import functools
import math

import jax
import jax.numpy as jnp
from jax import lax
from jax.experimental import pallas as pl
from jax.experimental.pallas import tpu as pltpu
from jax.sharding import PartitionSpec as P

MESH = pl.DeviceIdType.MESH
HD = 128
HEADS = 4
NEG = -1e30
SCALE = math.log2(math.e) / math.sqrt(HD)
GRID_Z = 4
BLOCK = 256


def nt_dot(a, b):
    return lax.dot_general(a, b, (((1,), (1,)), ((), ())), preferred_element_type=jnp.float32)


def nn_dot(a, b):
    return jnp.dot(a, b, preferred_element_type=jnp.float32)


def kernel(
    chips_z,
    plen_ref, scount_ref, slen_ref, owner_ref, dq_ref, skv_ref,
    prefix_hbm, pages_hbm, pq_hbm, pkv_hbm, w_hbm,
    dec_out, pre_out,
    prefix, pages, pq, pkv, w, po, kt, v1,
    table, table_sib, tab_s, tab_sib_s,
    q_all, acc_send, st_send, acc_recv, st_recv, part, rs_recv, dec,
    in_sem, out_sem, tab_sem, swap_send, swap_recv,
    q_send, q_recv, a_send, a_recv, t_send, t_recv, r_send, r_recv,
):
    span = pq.shape[0]
    pages_dev = pages_hbm.shape[0]
    samples = dq_ref.shape[0]
    rows = samples * HEADS
    chips = q_all.shape[0]
    chips_y = chips // chips_z
    n_t = rs_recv.shape[0]
    dp = lax.axis_index("dp")
    me_t = lax.axis_index("tensor")
    chip, core = dp // 2, dp % 2
    sibling = chip * 2 + (1 - core)
    my_y, my_z = chip // chips_z, chip % chips_z

    order = sorted(
        range(chips),
        key=lambda r: (min(r // chips_z, chips_y - r // chips_z) + 2 * min(r % chips_z, chips_z - r % chips_z), r),
    )

    def forward(r):
        return ((my_y + r // chips_z) % chips_y) * chips_z + (my_z + r % chips_z) % chips_z

    def backward(r):
        return ((my_y + chips_y - r // chips_z) % chips_y) * chips_z + (my_z + chips_z - r % chips_z) % chips_z

    barrier = pltpu.get_barrier_semaphore()
    for r in range(1, chips):
        pl.semaphore_signal(barrier, inc=1, device_id=(forward(r) * 2 + core, me_t), device_id_type=MESH)
    for u in range(1, n_t):
        pl.semaphore_signal(barrier, inc=1, device_id=(dp, (me_t + u) % n_t), device_id_type=MESH)
    pl.semaphore_signal(barrier, inc=1, device_id=(sibling, me_t), device_id_type=MESH)

    load_kv = pltpu.make_async_copy(pkv_hbm, pkv, in_sem.at[0])
    load_q = pltpu.make_async_copy(pq_hbm, pq, in_sem.at[1])
    load_prefix = pltpu.make_async_copy(prefix_hbm.at[0], prefix, in_sem.at[2])
    load_pages = pltpu.make_async_copy(pages_hbm, pages.at[pl.ds(0, pages_dev)], in_sem.at[3])
    load_w = pltpu.make_async_copy(w_hbm, w, in_sem.at[4])
    for copy in (load_kv, load_q, load_pages, load_prefix, load_w):
        copy.start()

    place = lax.broadcasted_iota(jnp.int32, (pages_dev, 128), 0)
    lane = lax.broadcasted_iota(jnp.int32, (pages_dev, 128), 1)
    hit = owner_ref[...] == lane
    first = jnp.min(jnp.where(hit, place, pages_dev), axis=0, keepdims=True)
    last = jnp.max(jnp.where(hit, place, -1), axis=0, keepdims=True)
    row8 = lax.broadcasted_iota(jnp.int32, (8, 128), 0)
    table[...] = jnp.where(row8 == 0, first, last)
    own_tab = pltpu.make_async_copy(table, tab_s, tab_sem.at[0])
    own_tab.start()

    load_kv.wait()
    ktt = pkv[:, :HD].T
    kt[:HD, :] = ktt
    kt[HD:, :] = ktt
    v1[:, :HD] = pkv[:, HD:]
    v1[:, HD:] = jnp.ones((span, HD), jnp.bfloat16)
    load_q.wait()
    length = slen_ref[0]
    block = min(BLOCK, span)
    n_blocks = span // block
    tri = lax.broadcasted_iota(jnp.int32, (block, block), 1) <= lax.broadcasted_iota(jnp.int32, (block, block), 0)

    def prefill(i):
        lo, nk = i * block, (i + 1) * block
        live = lo + lax.broadcasted_iota(jnp.int32, (block, HD), 0) < length
        for h in range(HEADS):
            q = pq[lo:nk, h * HD:(h + 1) * HD].astype(jnp.float32) * SCALE
            q_hi = q.astype(jnp.bfloat16)
            q_lo = (q - q_hi.astype(jnp.float32)).astype(jnp.bfloat16)
            s = nn_dot(jnp.concatenate([q_hi, q_lo], axis=1), kt[:, :nk])
            diag = jnp.where(tri, s[:, lo:], NEG)
            s = jnp.concatenate([s[:, :lo], diag], axis=1) if i else diag
            top = jnp.max(s, axis=1, keepdims=True)
            p = jnp.exp2(s - top).astype(jnp.bfloat16)
            o = nn_dot(p, v1[:nk, :])
            out = jnp.where(live, o[:, :HD] / o[:, HD:], 0.0)
            po[lo:nk, h * HD:(h + 1) * HD] = out.astype(jnp.bfloat16)
        pltpu.make_async_copy(po.at[pl.ds(lo, block)], pre_out.at[pl.ds(lo, block)], out_sem.at[i]).start()

    sequence = list(range(n_blocks))
    cut_a, cut_b, cut_c = 3 * n_blocks // 8, 5 * n_blocks // 8, 7 * n_blocks // 8
    for i in sequence[:cut_a]:
        prefill(i)

    pl.semaphore_wait(barrier, chips - 1 + n_t - 1 + 1)
    swap = [
        pltpu.make_async_remote_copy(
            table, table_sib, swap_send.at[0], swap_recv.at[0], device_id=(sibling, me_t), device_id_type=MESH),
        pltpu.make_async_remote_copy(
            pages_hbm, pages.at[pl.ds(pages_dev, pages_dev)], swap_send.at[1], swap_recv.at[1],
            device_id=(sibling, me_t), device_id_type=MESH),
    ]

    def q_copy(r):
        return pltpu.make_async_remote_copy(
            dq_ref, q_all.at[r], q_send.at[r], q_recv.at[r],
            device_id=(forward(r) * 2 + core, me_t), device_id_type=MESH)

    swap[0].start()
    for r in order[::-1]:
        if r:
            q_copy(r).start()
    swap[1].start()

    def stacked(x):
        return jnp.concatenate([x[:, h * HD:(h + 1) * HD] for h in range(HEADS)], axis=0)

    dq = stacked(dq_ref[...])
    load_prefix.wait()
    n_prefix = prefix.shape[0]
    s = nt_dot(dq, prefix[:, :HD]) * SCALE
    at = lax.broadcasted_iota(jnp.int32, (rows, n_prefix), 1)
    s = jnp.where(at < plen_ref[0], s, NEG)
    own_k = jnp.concatenate([skv_ref[:, :HD].astype(jnp.float32)] * HEADS, axis=0)
    own_v = jnp.concatenate([skv_ref[:, HD:].astype(jnp.float32)] * HEADS, axis=0)
    own_s = jnp.sum(dq.astype(jnp.float32) * own_k, axis=1, keepdims=True) * SCALE
    m_pre = jnp.maximum(jnp.max(s, axis=1, keepdims=True), own_s)
    p = jnp.exp2(s - m_pre)
    own_w = jnp.exp2(own_s - m_pre)
    l_pre = jnp.sum(p, axis=1, keepdims=True) + own_w
    acc_pre = nn_dot(p.astype(jnp.bfloat16), prefix[:, HD:])
    acc_pre = acc_pre + own_w.astype(jnp.bfloat16).astype(jnp.float32) * own_v

    for i in sequence[cut_a:cut_b]:
        prefill(i)

    load_pages.wait()
    own_tab.wait()
    swap[0].wait()
    sib_tab = pltpu.make_async_copy(table_sib, tab_sib_s, tab_sem.at[1])
    sib_tab.start()
    sib_tab.wait()
    swap[1].wait()
    ones = jnp.ones((pages.shape[1], HD), jnp.bfloat16)
    lane_r = lax.broadcasted_iota(jnp.int32, (rows, 128), 1)
    row_r = lax.broadcasted_iota(jnp.int32, (rows, 128), 0)

    def a_copy(r):
        return pltpu.make_async_remote_copy(
            acc_send.at[r], acc_recv.at[r], a_send.at[r], a_recv.at[r],
            device_id=(backward(r) * 2 + core, me_t), device_id_type=MESH)

    def t_copy(r):
        return pltpu.make_async_remote_copy(
            st_send.at[r], st_recv.at[r], t_send.at[r], t_recv.at[r],
            device_id=(backward(r) * 2 + core, me_t), device_id_type=MESH)

    def serve(r):
        q = stacked(q_all[r]) if r else dq
        prompt = backward(r) * 2 + core
        held = []
        for tab, base in ((tab_s, 0), (tab_sib_s, pages_dev)):
            a, b = tab[0, prompt], tab[1, prompt]
            held.append((base + jnp.minimum(a, pages_dev - 1), b >= a))
            held.append((base + jnp.maximum(b, 0), b > a))
        kvs = [pages[index] for index, _ in held]
        s = jnp.concatenate(
            [nt_dot(q, kv[:, :HD]) * SCALE + jnp.where(valid, 0.0, NEG)
             for kv, (_, valid) in zip(kvs, held)], axis=1)
        m = jnp.max(s, axis=1, keepdims=True)
        p = jnp.exp2(s - m).astype(jnp.bfloat16)
        v = jnp.concatenate([jnp.concatenate([kv[:, HD:], ones], axis=1) for kv in kvs], axis=0)
        o = nn_dot(p, v)
        stat = jnp.where(lane_r == row_r, m, jnp.where(lane_r == row_r + rows, o[:, HD:], 0.0))
        stat = jnp.sum(stat, axis=0, keepdims=True)
        if r:
            acc_send[r] = o[:, :HD].astype(jnp.bfloat16)
            st_send[r] = stat
        else:
            acc_recv[0] = o[:, :HD].astype(jnp.bfloat16)
            st_recv[0] = stat

    for start in range(0, chips, 4):
        group = order[start:start + 4]
        for r in group:
            if r:
                q_copy(r).wait_recv()
        for r in group:
            serve(r)
        for r in group:
            if r:
                t_copy(r).start()
                a_copy(r).start()

    for i in sequence[cut_c:] + sequence[cut_b:cut_c - 1]:
        prefill(i)

    for r in range(1, chips):
        t_copy(r).wait_recv()
        a_copy(r).wait_recv()
    stats = jnp.concatenate([st_recv[r] for r in range(chips)], axis=0).T
    m_all, l_all = stats[:rows, :], stats[rows:2 * rows, :]
    m_top = jnp.maximum(jnp.max(m_all, axis=1, keepdims=True), m_pre)
    w_all = jnp.exp2(m_all - m_top)
    w_pre = jnp.exp2(m_pre - m_top)
    total = jnp.sum(l_all * w_all, axis=1, keepdims=True) + l_pre * w_pre
    acc = acc_pre * w_pre
    for r in range(chips):
        acc = acc + acc_recv[r].astype(jnp.float32) * w_all[:, r:r + 1]
    att = (acc / total).astype(jnp.bfloat16)
    att = jnp.concatenate([att[h * samples:(h + 1) * samples, :] for h in range(HEADS)], axis=1)

    load_w.wait()
    wide = dec.shape[1]
    for b in range(n_t):
        part[b] = nn_dot(att, w[:, b * wide:(b + 1) * wide]).astype(jnp.bfloat16)

    def r_copy(u):
        to = (me_t + u) % n_t
        return pltpu.make_async_remote_copy(
            part.at[to], rs_recv.at[u], r_send.at[u], r_recv.at[u], device_id=(dp, to), device_id_type=MESH)

    for u in range(1, n_t):
        r_copy(u).start()

    for i in sequence[cut_c - 1:cut_c]:
        prefill(i)

    sums = part[me_t].astype(jnp.float32)
    for u in range(1, n_t):
        r_copy(u).wait_recv()
        sums = sums + rs_recv[u].astype(jnp.float32)
    alive = lax.broadcasted_iota(jnp.int32, sums.shape, 0) < scount_ref[0]
    dec[...] = jnp.where(alive, sums, 0.0).astype(jnp.bfloat16)
    store = pltpu.make_async_copy(dec, dec_out, out_sem.at[n_blocks])
    store.start()

    for r in range(1, chips):
        q_copy(r).wait_send()
        t_copy(r).wait_send()
        a_copy(r).wait_send()
    for u in range(1, n_t):
        r_copy(u).wait_send()
    for i in range(n_blocks):
        pltpu.make_async_copy(
            po.at[pl.ds(i * block, block)], pre_out.at[pl.ds(i * block, block)], out_sem.at[i]).wait()
    store.wait()


def solution(mesh, chips_z=GRID_Z):
    chips = mesh.shape["dp"] // 2
    n_t = mesh.shape["tensor"]

    def body(prefix_cache, prefix_len, decode_q, sample_kv, sample_count, sectioned_pages, page_owner,
             prefill_q, prefill_kv, span_len, out_weight):
        n_prefix, wide_kv = prefix_cache.shape[1:]
        pages_dev, page, _ = sectioned_pages.shape
        span, wide_q = prefill_q.shape
        samples = decode_q.shape[0]
        rows = samples * HEADS
        features = out_weight.shape[1]
        bf, f32 = jnp.bfloat16, jnp.float32
        n_blocks = span // min(BLOCK, span)
        vmem, smem, hbm = (pl.BlockSpec(memory_space=m) for m in (pltpu.VMEM, pltpu.SMEM, pl.ANY))
        dma, vm = pltpu.SemaphoreType.DMA, pltpu.VMEM
        return pl.pallas_call(
            functools.partial(kernel, chips_z),
            out_shape=(
                jax.ShapeDtypeStruct((samples, features // n_t), bf),
                jax.ShapeDtypeStruct((span, wide_q), bf),
            ),
            in_specs=[smem] * 3 + [vmem] * 3 + [hbm] * 5,
            out_specs=(hbm, hbm),
            scratch_shapes=[
                vm((n_prefix, wide_kv), bf), vm((2 * pages_dev, page, wide_kv), bf),
                vm((span, wide_q), bf), vm((span, wide_kv), bf), vm(out_weight.shape, bf),
                vm((span, wide_q), bf), vm((2 * HD, span), bf), vm((span, 2 * HD), bf),
                vm((8, 128), jnp.int32), vm((8, 128), jnp.int32),
                pltpu.SMEM((8, 128), jnp.int32), pltpu.SMEM((8, 128), jnp.int32),
                vm((chips, samples, wide_q), bf), vm((chips, rows, HD), bf), vm((chips, 1, 128), f32),
                vm((chips, rows, HD), bf), vm((chips, 1, 128), f32),
                vm((n_t, samples, features // n_t), bf), vm((n_t, samples, features // n_t), bf),
                vm((samples, features // n_t), bf),
                dma((5,)), dma((n_blocks + 1,)), dma((2,)), dma((2,)), dma((2,)),
                dma((chips,)), dma((chips,)), dma((chips,)), dma((chips,)), dma((chips,)), dma((chips,)),
                dma((n_t,)), dma((n_t,)),
            ],
            compiler_params=pltpu.CompilerParams(
                collective_id=0, has_side_effects=True, vmem_limit_bytes=50 * 2**20),
            cost_estimate=pl.CostEstimate(flops=6 * 10**9, bytes_accessed=12 * 2**20, transcendentals=10**7),
        )(prefix_len, sample_count, span_len, page_owner, decode_q, sample_kv,
          prefix_cache, sectioned_pages, prefill_q, prefill_kv, out_weight)

    in_specs = (
        P("dp", None, "tensor"), P("dp"), P("dp", "tensor"), P("dp", "tensor"), P("dp"),
        P("dp", None, "tensor"), P("dp", None), P("dp", "tensor"), P("dp", "tensor"), P("dp"), P("tensor", None),
    )
    out_specs = (P("dp", "tensor"), P("dp", "tensor"))
    return jax.shard_map(body, mesh=mesh, in_specs=in_specs, out_specs=out_specs, check_vma=False)
```

profile of v0, /device:TPU:1, one launch (start us, length us, event | category | flops | bytes accessed | tf_op | source)
XLA Modules:
  0.0 51.4 jit_solution(11125339399294951775)
XLA Ops:
  2.6 0.7 %copy.13.owner_ref = s32[24,1]{1,0:T(8,128)S(1)} copy(s32[24,1]{0,1:T(1,128)} %param.17) | data formatting | bytes 192 | tf_op args[6]
  3.3 0.0 copy-start
  3.3 1.4 %copy-done = bf16[24,128,256]{2,1,0:T(8,128)(2,1)S(1)} copy-done((bf16[24,128,256]{2,1,0:T(8,128)(2,1)S(1)}, bf16[24,128,256]{2,1,0:T(8,128)(2,1)}, u32[]{:S(2)}) %copy-start) | copy-done | bytes 1572888
  4.7 0.0 copy-start.1
  4.7 1.2 %copy-done.1 = bf16[1,2048,256]{2,1,0:T(8,128)(2,1)S(1)} copy-done((bf16[1,2048,256]{2,1,0:T(8,128)(2,1)S(1)}, bf16[1,2048,256]{2,1,0:T(8,128)(2,1)}, u32[]{:S(2)}) %copy-start.1) | copy-done | bytes 1048600
  5.9 0.0 copy-start.2
  5.9 1.2 %copy-done.2 = bf16[2048,256]{1,0:T(8,128)(2,1)S(1)} copy-done((bf16[2048,256]{1,0:T(8,128)(2,1)S(1)}, bf16[2048,256]{1,0:T(8,128)(2,1)}, u32[]{:S(2)}) %copy-start.2) | copy-done | bytes 1048600
  7.2 0.0 copy-start.3
  7.2 0.7 %copy-done.3 = bf16[16,512]{1,0:T(8,128)(2,1)S(1)} copy-done((bf16[16,512]{1,0:T(8,128)(2,1)S(1)}, bf16[16,512]{1,0:T(8,128)(2,1)}, u32[]{:S(2)}) %copy-start.3) | copy-done | bytes 16408
  7.9 0.0 copy-start.4
  7.9 0.7 %copy-done.4 = bf16[16,256]{1,0:T(8,128)(2,1)S(1)} copy-done((bf16[16,256]{1,0:T(8,128)(2,1)S(1)}, bf16[16,256]{1,0:T(8,128)(2,1)}, u32[]{:S(2)}) %copy-start.4) | copy-done | bytes 8216
  8.6 39.2 %shard_map.122 = (bf16[16,512]{1,0:T(8,128)(2,1)S(1)}, bf16[2048,512]{1,0:T(8,128)(2,1)}) custom-call(s32[1]{0:T(128)S(6)} %copy.16.plen_ref, s32[1]{0:T(128)S(6)} %copy.17.scount_ref, s32[1]{0:T(128)S(6)} %copy.18.slen_ref, s32[24,1]{1,0:T(8,128)S(1)} %copy.13.owner_ref, bf16[16,512]{1,0:T(8,128)(2,1)S(1)} %copy-done.3, bf16[16,256]{1,0:T(8,128)(2,1)S(1)} %copy-done.4, ...), custom_call_target="tpu_custom_call" | custom-call | flops 6000000000 | bytes 12582912 | tf_op jit(solution)/shard_map/pallas_call | solution.py:293
  47.8 0.6 %copy.19 = bf16[16,512]{1,0:T(8,128)(2,1)} copy(bf16[16,512]{1,0:T(8,128)(2,1)S(1)} %get-tuple-element.4) | data formatting | bytes 32768
  48.4 3.0 %copy.20 = bf16[2048,512]{1,0:T(8,128)(2,1)} copy(bf16[2048,512]{1,0:T(8,128)(2,1)} %get-tuple-element.5) | data formatting | bytes 4194304
Async XLA Ops:
  3.3 1.4 %copy-start = (bf16[24,128,256]{2,1,0:T(8,128)(2,1)S(1)}, bf16[24,128,256]{2,1,0:T(8,128)(2,1)}, u32[]{:S(2)}) copy-start(bf16[24,128,256]{2,1,0:T(8,128)(2,1)} %pages_hbm.1) | copy-start | bytes 4718596
  4.7 1.2 %copy-start.1 = (bf16[1,2048,256]{2,1,0:T(8,128)(2,1)S(1)}, bf16[1,2048,256]{2,1,0:T(8,128)(2,1)}, u32[]{:S(2)}) copy-start(bf16[1,2048,256]{2,1,0:T(8,128)(2,1)} %prefix_hbm.1) | copy-start | bytes 3145732
  5.9 1.2 %copy-start.2 = (bf16[2048,256]{1,0:T(8,128)(2,1)S(1)}, bf16[2048,256]{1,0:T(8,128)(2,1)}, u32[]{:S(2)}) copy-start(bf16[2048,256]{1,0:T(8,128)(2,1)} %pkv_hbm.1) | copy-start | bytes 3145732
  7.2 0.7 %copy-start.3 = (bf16[16,512]{1,0:T(8,128)(2,1)S(1)}, bf16[16,512]{1,0:T(8,128)(2,1)}, u32[]{:S(2)}) copy-start(bf16[16,512]{1,0:T(8,128)(2,1)} %dq_ref.1) | copy-start | bytes 49156
  7.9 0.7 %copy-start.4 = (bf16[16,256]{1,0:T(8,128)(2,1)S(1)}, bf16[16,256]{1,0:T(8,128)(2,1)}, u32[]{:S(2)}) copy-start(bf16[16,256]{1,0:T(8,128)(2,1)} %skv_ref.1) | copy-start | bytes 24580
where the time goes:
time: 51.8 us; the launch traced here: 51.4 us
  Pallas kernels  39.2 us (76%)
  local copies, waits for them, and re-layouts  9.66 us (19%)
  between operations  2.58 us (5%)
    pallas_call x1, Pallas kernels, body(): pl.pallas_call(functools.partial(kernel, chips_z), out_shape=(jax.ShapeDt...  39.2 us
    unnamed x13, local copies, waits for them, and re-layouts  9.66 us

commit v1 on v0

v1 whole, which is shorter than its diff:
```python
import functools
import math

import jax
import jax.numpy as jnp
from jax import lax
from jax.experimental import pallas as pl
from jax.experimental.pallas import tpu as pltpu
from jax.sharding import PartitionSpec as P

MESH = pl.DeviceIdType.MESH
HD = 128
HEADS = 4
NEG = -1e30
SCALE = math.log2(math.e) / math.sqrt(HD)
GRID_Z = 4
BLOCK = 256


def nt_dot(a, b):
    return lax.dot_general(a, b, (((1,), (1,)), ((), ())), preferred_element_type=jnp.float32)


def nn_dot(a, b):
    return jnp.dot(a, b, preferred_element_type=jnp.float32)


def kernel(
    chips_z,
    plen_hbm, scount_hbm, slen_hbm, owner_hbm, dq_hbm, skv_hbm,
    prefix_hbm, pages_hbm, pq_hbm, pkv_hbm, w_hbm,
    dec, po,
    plen_ref, scount_ref, slen_ref, owner_ref, dq_ref, skv_ref,
    prefix, pages, pq, pkv, w, kt, v1,
    table, table_sib, tab_s, tab_sib_s,
    q_all, acc_send, st_send, acc_recv, st_recv, part, rs_recv,
    in_sem, tab_sem, swap_send, swap_recv,
    q_send, q_recv, a_send, a_recv, t_send, t_recv, r_send, r_recv,
):
    span = pq.shape[0]
    pages_dev = pages_hbm.shape[0]
    samples = dq_ref.shape[0]
    rows = samples * HEADS
    chips = q_all.shape[0]
    chips_y = chips // chips_z
    n_t = rs_recv.shape[0]
    dp = lax.axis_index("dp")
    me_t = lax.axis_index("tensor")
    chip, core = dp // 2, dp % 2
    sibling = chip * 2 + (1 - core)
    my_y, my_z = chip // chips_z, chip % chips_z

    early_waves, late_waves = list(range(chips_z // 2)), list(range(chips_z // 2, chips_z))
    is_first = my_z == 0
    is_early = my_z < chips_z // 2
    is_late = my_z >= chips_z // 2

    def chip_at(k, z):
        return ((my_y + k) % chips_y) * chips_z + z

    def remote(k, z, action):
        if k:
            action(chip_at(k, z))
        else:
            pl.when(my_z != z)(lambda: action(chip_at(k, z)))

    far_first = sorted(range(chips_y), key=lambda k: -min(k, chips_y - k))
    everywhere = [(k, z) for z in late_waves + early_waves for k in far_first]

    barrier = pltpu.get_barrier_semaphore()
    for k, z in everywhere:
        remote(k, z, lambda to: pl.semaphore_signal(
            barrier, inc=1, device_id=(to * 2 + core, me_t), device_id_type=MESH))
    for u in range(1, n_t):
        pl.semaphore_signal(barrier, inc=1, device_id=(dp, (me_t + u) % n_t), device_id_type=MESH)
    pl.semaphore_signal(barrier, inc=1, device_id=(sibling, me_t), device_id_type=MESH)

    load_kv = pltpu.make_async_copy(pkv_hbm, pkv, in_sem.at[0])
    load_q = pltpu.make_async_copy(pq_hbm, pq, in_sem.at[1])
    load_prefix = pltpu.make_async_copy(prefix_hbm.at[0], prefix, in_sem.at[2])
    load_pages = pltpu.make_async_copy(pages_hbm, pages.at[pl.ds(0, pages_dev)], in_sem.at[3])
    load_w = pltpu.make_async_copy(w_hbm, w, in_sem.at[4])
    small = [
        pltpu.make_async_copy(src, dst, in_sem.at[5 + i])
        for i, (src, dst) in enumerate((
            (owner_hbm, owner_ref), (slen_hbm, slen_ref), (dq_hbm, dq_ref), (skv_hbm, skv_ref),
            (plen_hbm, plen_ref), (scount_hbm, scount_ref)))
    ]
    load_owner, load_slen, load_dq, load_skv, load_plen, load_scount = small
    for copy in (load_owner, load_slen, load_kv, load_dq, load_q, load_pages, load_skv, load_plen, load_prefix,
                 load_scount, load_w):
        copy.start()

    load_owner.wait()
    prompts = table.shape[0]
    place = lax.broadcasted_iota(jnp.int32, (prompts, pages_dev), 1).astype(jnp.float32)
    prompt_at = lax.broadcasted_iota(jnp.int32, (prompts, pages_dev), 0)
    hit = jnp.broadcast_to(owner_ref[...], (prompts, pages_dev)) == prompt_at
    first = jnp.min(jnp.where(hit, place, float(pages_dev)), axis=1, keepdims=True)
    last = jnp.max(jnp.where(hit, place, -1.0), axis=1, keepdims=True)
    column = lax.broadcasted_iota(jnp.int32, (prompts, 128), 1)
    table[...] = jnp.where(column == 0, first, last).astype(jnp.int32)
    own_tab = pltpu.make_async_copy(table, tab_s, tab_sem.at[0])
    own_tab.start()

    block = min(BLOCK, span)
    n_blocks = span // block
    tri = lax.broadcasted_iota(jnp.int32, (block, block), 1) <= lax.broadcasted_iota(jnp.int32, (block, block), 0)

    def prepare():
        load_kv.wait()
        load_q.wait()
        load_slen.wait()
        ktt = pkv[:, :HD].T
        kt[:HD, :] = ktt
        kt[HD:, :] = ktt
        v1[:, :HD] = pkv[:, HD:]
        v1[:, HD:] = jnp.ones((span, HD), jnp.bfloat16)

    def prefill(i):
        lo, nk = i * block, (i + 1) * block
        length = jnp.broadcast_to(slen_ref[...], (block, HD))
        live = lo + lax.broadcasted_iota(jnp.int32, (block, HD), 0) < length
        for h in range(HEADS):
            q = pq[lo:nk, h * HD:(h + 1) * HD].astype(jnp.float32) * SCALE
            q_hi = q.astype(jnp.bfloat16)
            q_lo = (q - q_hi.astype(jnp.float32)).astype(jnp.bfloat16)
            s = nn_dot(jnp.concatenate([q_hi, q_lo], axis=1), kt[:, :nk])
            diag = jnp.where(tri, s[:, lo:], NEG)
            s = jnp.concatenate([s[:, :lo], diag], axis=1) if i else diag
            top = jnp.max(s, axis=1, keepdims=True)
            p = jnp.exp2(s - top).astype(jnp.bfloat16)
            o = nn_dot(p, v1[:nk, :])
            out = jnp.where(live, o[:, :HD] / o[:, HD:], 0.0)
            po[lo:nk, h * HD:(h + 1) * HD] = out.astype(jnp.bfloat16)

    def prefills(when, blocks):
        def run():
            for i in blocks:
                prefill(i)
        pl.when(when)(run)

    prepare()
    for i in (0, 1):
        prefill(i)

    pl.semaphore_wait(barrier, chips - 1 + n_t - 1 + 1)
    load_dq.wait()
    swap = [
        pltpu.make_async_remote_copy(
            table, table_sib, swap_send.at[0], swap_recv.at[0], device_id=(sibling, me_t), device_id_type=MESH),
        pltpu.make_async_remote_copy(
            pages_hbm, pages.at[pl.ds(pages_dev, pages_dev)], swap_send.at[1], swap_recv.at[1],
            device_id=(sibling, me_t), device_id_type=MESH),
    ]

    def q_copy(to, slot):
        return pltpu.make_async_remote_copy(
            dq_ref, q_all.at[slot], q_send.at[to], q_recv.at[slot],
            device_id=(to * 2 + core, me_t), device_id_type=MESH)

    def send_queries():
        for k, z in everywhere:
            remote(k, z, lambda to: q_copy(to, chip).start())

    swap[0].start()
    send_queries()
    swap[1].start()
    q_all[chip] = dq_ref[...]

    def stacked(x):
        return jnp.concatenate([x[:, h * HD:(h + 1) * HD] for h in range(HEADS)], axis=0)

    dq = stacked(dq_ref[...])
    load_prefix.wait()
    load_skv.wait()
    load_plen.wait()
    n_prefix = prefix.shape[0]
    s = nt_dot(dq, prefix[:, :HD]) * SCALE
    at = lax.broadcasted_iota(jnp.int32, (rows, n_prefix), 1)
    s = jnp.where(at < jnp.broadcast_to(plen_ref[...], (rows, n_prefix)), s, NEG)
    own_k = jnp.concatenate([skv_ref[:, :HD].astype(jnp.float32)] * HEADS, axis=0)
    own_v = jnp.concatenate([skv_ref[:, HD:].astype(jnp.float32)] * HEADS, axis=0)
    own_s = jnp.sum(dq.astype(jnp.float32) * own_k, axis=1, keepdims=True) * SCALE
    m_pre = jnp.maximum(jnp.max(s, axis=1, keepdims=True), own_s)
    p = jnp.exp2(s - m_pre)
    own_w = jnp.exp2(own_s - m_pre)
    l_pre = jnp.sum(p, axis=1, keepdims=True) + own_w
    acc_pre = nn_dot(p.astype(jnp.bfloat16), prefix[:, HD:])
    acc_pre = acc_pre + own_w.astype(jnp.bfloat16).astype(jnp.float32) * own_v

    for i in (2, 3, 4):
        prefill(i)

    load_pages.wait()
    own_tab.wait()
    swap[0].wait()
    sib_tab = pltpu.make_async_copy(table_sib, tab_sib_s, tab_sem.at[1])
    sib_tab.start()
    sib_tab.wait()
    swap[1].wait()
    ones = jnp.ones((pages.shape[1], HD), jnp.bfloat16)
    lane_r = lax.broadcasted_iota(jnp.int32, (rows, 128), 1)
    row_r = lax.broadcasted_iota(jnp.int32, (rows, 128), 0)

    def a_copy(to, slot):
        return pltpu.make_async_remote_copy(
            acc_send.at[to], acc_recv.at[slot], a_send.at[to], a_recv.at[slot],
            device_id=(to * 2 + core, me_t), device_id_type=MESH)

    def t_copy(to, slot):
        return pltpu.make_async_remote_copy(
            st_send.at[to], st_recv.at[slot], t_send.at[to], t_recv.at[slot],
            device_id=(to * 2 + core, me_t), device_id_type=MESH)

    def serve(r):
        q = stacked(q_all[r])
        prompt = r * 2 + core
        held = []
        for tab, base in ((tab_s, 0), (tab_sib_s, pages_dev)):
            a, b = tab[prompt, 0], tab[prompt, 1]
            held.append((base + jnp.clip(a, 0, pages_dev - 1), b >= a))
            held.append((base + jnp.clip(b, 0, pages_dev - 1), b > a))
        kvs = [pages[index] for index, _ in held]
        s = jnp.concatenate(
            [nt_dot(q, kv[:, :HD]) * SCALE + jnp.where(valid, 0.0, NEG)
             for kv, (_, valid) in zip(kvs, held)], axis=1)
        m = jnp.max(s, axis=1, keepdims=True)
        p = jnp.exp2(s - m).astype(jnp.bfloat16)
        v = jnp.concatenate([jnp.concatenate([kv[:, HD:], ones], axis=1) for kv in kvs], axis=0)
        o = nn_dot(p, v)
        stat = jnp.where(lane_r == row_r, m, jnp.where(lane_r == row_r + rows, o[:, HD:], 0.0))
        stat = jnp.sum(stat, axis=0, keepdims=True)
        acc_send[r] = o[:, :HD].astype(jnp.bfloat16)
        st_send[r] = stat

    for z in early_waves + late_waves:
        for k in far_first:
            remote(k, z, lambda of: q_copy(of, of).wait_recv())
        for k in far_first:
            serve(chip_at(k, z))
        for k in far_first:
            remote(k, z, lambda to: t_copy(to, chip).start())
            remote(k, z, lambda to: a_copy(to, chip).start())
    acc_recv[chip] = acc_send[chip]
    st_recv[chip] = st_send[chip]
    for i in (5, 7):
        prefill(i)

    for k, z in everywhere:
        remote(k, z, lambda of: t_copy(of, of).wait_recv())
        remote(k, z, lambda of: a_copy(of, of).wait_recv())
    stats = jnp.concatenate([st_recv[r] for r in range(chips)], axis=0).T
    m_all, l_all = stats[:rows, :], stats[rows:2 * rows, :]
    m_top = jnp.maximum(jnp.max(m_all, axis=1, keepdims=True), m_pre)
    w_all = jnp.exp2(m_all - m_top)
    w_pre = jnp.exp2(m_pre - m_top)
    total = jnp.sum(l_all * w_all, axis=1, keepdims=True) + l_pre * w_pre
    acc = acc_pre * w_pre
    for r in range(chips):
        acc = acc + acc_recv[r].astype(jnp.float32) * w_all[:, r:r + 1]
    att = (acc / total).astype(jnp.bfloat16)
    att = jnp.concatenate([att[h * samples:(h + 1) * samples, :] for h in range(HEADS)], axis=1)

    load_w.wait()
    wide = dec.shape[1]

    def product(u):
        to = (me_t + u) % n_t
        return nn_dot(att, w[:, pl.ds(pl.multiple_of(to * wide, wide), wide)])

    def r_copy(u):
        return pltpu.make_async_remote_copy(
            part.at[u], rs_recv.at[u], r_send.at[u], r_recv.at[u],
            device_id=(dp, (me_t + u) % n_t), device_id_type=MESH)

    for u in range(1, n_t):
        part[u] = product(u).astype(jnp.bfloat16)
        r_copy(u).start()
    part[0] = product(0).astype(jnp.bfloat16)

    for i in (6,):
        prefill(i)

    sums = part[0].astype(jnp.float32)
    for u in range(1, n_t):
        r_copy(u).wait_recv()
        sums = sums + rs_recv[u].astype(jnp.float32)
    load_scount.wait()
    alive = lax.broadcasted_iota(jnp.int32, sums.shape, 0) < jnp.broadcast_to(scount_ref[...], sums.shape)
    dec[...] = jnp.where(alive, sums, 0.0).astype(jnp.bfloat16)

    for k, z in everywhere:
        remote(k, z, lambda to: q_copy(to, chip).wait_send())
        remote(k, z, lambda to: t_copy(to, chip).wait_send())
        remote(k, z, lambda to: a_copy(to, chip).wait_send())
    for u in range(1, n_t):
        r_copy(u).wait_send()


def store(dec, pre, dec_out, pre_out, sem):
    copies = [pltpu.make_async_copy(pre, pre_out, sem.at[0]), pltpu.make_async_copy(dec, dec_out, sem.at[1])]
    for copy in copies:
        copy.start()
    for copy in copies:
        copy.wait()


def solution(mesh, chips_z=GRID_Z):
    chips = mesh.shape["dp"] // 2
    n_t = mesh.shape["tensor"]

    def body(prefix_cache, prefix_len, decode_q, sample_kv, sample_count, sectioned_pages, page_owner,
             prefill_q, prefill_kv, span_len, out_weight):
        n_prefix, wide_kv = prefix_cache.shape[1:]
        pages_dev, page, _ = sectioned_pages.shape
        span, wide_q = prefill_q.shape
        samples = decode_q.shape[0]
        rows = samples * HEADS
        features = out_weight.shape[1]
        bf, f32 = jnp.bfloat16, jnp.float32
        hbm = pl.BlockSpec(memory_space=pltpu.HBM)
        prompts = mesh.shape["dp"]
        dma, vm = pltpu.SemaphoreType.DMA, pltpu.VMEM
        outs = pl.pallas_call(
            functools.partial(kernel, chips_z),
            out_shape=(
                vm((samples, features // n_t), bf),
                vm((span, wide_q), bf),
            ),
            in_specs=[hbm] * 11,
            out_specs=(pl.BlockSpec(memory_space=vm),) * 2,
            scratch_shapes=[
                vm((1, 1), jnp.int32), vm((1, 1), jnp.int32), vm((1, 1), jnp.int32),
                vm((1, pages_dev), jnp.int32), vm((samples, wide_q), bf), vm((samples, wide_kv), bf),
                vm((n_prefix, wide_kv), bf), vm((2 * pages_dev, page, wide_kv), bf),
                vm((span, wide_q), bf), vm((span, wide_kv), bf), vm(out_weight.shape, bf),
                vm((2 * HD, span), bf), vm((span, 2 * HD), bf),
                vm((prompts, 128), jnp.int32), vm((prompts, 128), jnp.int32),
                pltpu.SMEM((prompts, 128), jnp.int32), pltpu.SMEM((prompts, 128), jnp.int32),
                vm((chips, samples, wide_q), bf), vm((chips, rows, HD), bf), vm((chips, 1, 128), f32),
                vm((chips, rows, HD), bf), vm((chips, 1, 128), f32),
                vm((n_t, samples, features // n_t), bf), vm((n_t, samples, features // n_t), bf),
                dma((11,)), dma((2,)), dma((2,)), dma((2,)),
                dma((chips,)), dma((chips,)), dma((chips,)), dma((chips,)), dma((chips,)), dma((chips,)),
                dma((n_t,)), dma((n_t,)),
            ],
            compiler_params=pltpu.CompilerParams(
                collective_id=0, has_side_effects=True, vmem_limit_bytes=56 * 2**20),
            cost_estimate=pl.CostEstimate(flops=6 * 10**9, bytes_accessed=12 * 2**20, transcendentals=10**7),
        )(prefix_len[None], sample_count[None], span_len[None], page_owner.T, decode_q, sample_kv,
          prefix_cache, sectioned_pages, prefill_q, prefill_kv, out_weight)
        return pl.pallas_call(
            store,
            out_shape=tuple(jax.ShapeDtypeStruct(out.shape, out.dtype) for out in outs),
            in_specs=[pl.BlockSpec(memory_space=vm)] * 2,
            out_specs=(hbm, hbm),
            scratch_shapes=[dma((2,))],
        )(*(pltpu.with_memory_space_constraint(out, vm) for out in outs))

    in_specs = (
        P("dp", None, "tensor"), P("dp"), P("dp", "tensor"), P("dp", "tensor"), P("dp"),
        P("dp", None, "tensor"), P("dp", None), P("dp", "tensor"), P("dp", "tensor"), P("dp"), P("tensor", None),
    )
    out_specs = (P("dp", "tensor"), P("dp", "tensor"))
    return jax.shard_map(body, mesh=mesh, in_specs=in_specs, out_specs=out_specs, check_vma=False)
```

time: 51.8 us -> 39.4 us (0.76)
  local copies, waits for them, and re-layouts: 9.66 us -> 0 us
  Pallas kernels: 39.2 us -> 36.1 us
    unnamed x13 -> x0, local copies, waits for them, and re-layouts: 9.66 us -> none
    pallas_call x1 -> x2, Pallas kernels: 39.2 us -> 36.1 us  [the longest x1 34.7 us: body(): pl.pallas_call(functools.partial(kernel, chips_z), out_shape=(vm((samples...]
where the time goes in v1:
time: 39.4 us; the launch traced here: 38.8 us
  Pallas kernels  36.1 us (92%)
  between operations  2.74 us (7%)
    pallas_call x1, Pallas kernels, body(): pl.pallas_call(functools.partial(kernel, chips_z), out_shape=(vm((samples...  34.7 us
    pallas_call x1, Pallas kernels, body(): pl.pallas_call(store, out_shape=tuple((jax.ShapeDtypeStruct(out.shape, ou...  1.34 us

profile of v1, /device:TPU:1, one launch (start us, length us, event | category | flops | bytes accessed | tf_op | source)
XLA Modules:
  0.0 38.8 jit_solution(8793314023130353060)
XLA Ops:
  2.6 34.7 %shard_map.122 = (bf16[16,512]{1,0:T(8,128)(2,1)S(1)}, bf16[2048,512]{1,0:T(8,128)(2,1)S(1)}) custom-call(s32[1,1]{1,0:T(1,128)} %bitcast.4.plen_hbm, s32[1,1]{1,0:T(1,128)} %bitcast.5.scount_hbm, s32[1,1]{1,0:T(1,128)} %bitcast.6.slen_hbm, s32[1,24]{1,0:T(1,128)} %bitcast.7, bf16[16,512]{1,0:T(8,128)(2,1)} %dq_hbm.1, bf16[16,256]{1,0:T(8,128)(2,1)} %skv_hbm.1, ...), custom_call_target="tpu_custom_call" | custom-call | flops 6000000000 | bytes 12582912 | tf_op jit(solution)/shard_map/pallas_call | solution.py:325
  37.3 1.3 %shard_map.123 = (bf16[16,512]{1,0:T(8,128)(2,1)}, bf16[2048,512]{1,0:T(8,128)(2,1)}) custom-call(bf16[16,512]{1,0:T(8,128)(2,1)S(1)} %get-tuple-element.4.dec, bf16[2048,512]{1,0:T(8,128)(2,1)S(1)} %get-tuple-element.5.pre), custom_call_target="tpu_custom_call" | custom-call | tf_op jit(solution)/shard_map/pallas_call | solution.py:353

commit v2 on v1

--- a/solution.py
+++ b/solution.py
@@ -117,32 +117,34 @@
         v1[:, :HD] = pkv[:, HD:]
         v1[:, HD:] = jnp.ones((span, HD), jnp.bfloat16)
 
-    def prefill(i):
+    def scores(i, h):
         lo, nk = i * block, (i + 1) * block
-        length = jnp.broadcast_to(slen_ref[...], (block, HD))
-        live = lo + lax.broadcasted_iota(jnp.int32, (block, HD), 0) < length
-        for h in range(HEADS):
-            q = pq[lo:nk, h * HD:(h + 1) * HD].astype(jnp.float32) * SCALE
-            q_hi = q.astype(jnp.bfloat16)
-            q_lo = (q - q_hi.astype(jnp.float32)).astype(jnp.bfloat16)
-            s = nn_dot(jnp.concatenate([q_hi, q_lo], axis=1), kt[:, :nk])
-            diag = jnp.where(tri, s[:, lo:], NEG)
-            s = jnp.concatenate([s[:, :lo], diag], axis=1) if i else diag
-            top = jnp.max(s, axis=1, keepdims=True)
-            p = jnp.exp2(s - top).astype(jnp.bfloat16)
-            o = nn_dot(p, v1[:nk, :])
-            out = jnp.where(live, o[:, :HD] / o[:, HD:], 0.0)
-            po[lo:nk, h * HD:(h + 1) * HD] = out.astype(jnp.bfloat16)
-
-    def prefills(when, blocks):
-        def run():
-            for i in blocks:
-                prefill(i)
-        pl.when(when)(run)
+        q = pq[lo:nk, h * HD:(h + 1) * HD].astype(jnp.float32) * SCALE
+        q_hi = q.astype(jnp.bfloat16)
+        q_lo = (q - q_hi.astype(jnp.float32)).astype(jnp.bfloat16)
+        return nn_dot(jnp.concatenate([q_hi, q_lo], axis=1), kt[:, :nk])
+
+    def finish(i, h, s):
+        lo, nk = i * block, (i + 1) * block
+        diag = jnp.where(tri, s[:, lo:], NEG)
+        s = jnp.concatenate([s[:, :lo], diag], axis=1) if i else diag
+        top = jnp.max(s, axis=1, keepdims=True)
+        p = jnp.exp2(s - top).astype(jnp.bfloat16)
+        o = nn_dot(p, v1[:nk, :])
+        live = lo + lax.broadcasted_iota(jnp.int32, (block, HD), 0) < jnp.broadcast_to(slen_ref[...], (block, HD))
+        out = jnp.where(live, o[:, :HD] / o[:, HD:], 0.0)
+        po[lo:nk, h * HD:(h + 1) * HD] = out.astype(jnp.bfloat16)
+
+    def prefill(*blocks):
+        units = [(i, h) for i in blocks for h in range(HEADS)]
+        s = scores(*units[0])
+        for unit, later in zip(units, units[1:] + [None]):
+            ahead = scores(*later) if later else None
+            finish(*unit, s)
+            s = ahead
 
     prepare()
-    for i in (0, 1):
-        prefill(i)
+    prefill(0, 1)
 
     pl.semaphore_wait(barrier, chips - 1 + n_t - 1 + 1)
     load_dq.wait()
@@ -189,8 +191,7 @@
     acc_pre = nn_dot(p.astype(jnp.bfloat16), prefix[:, HD:])
     acc_pre = acc_pre + own_w.astype(jnp.bfloat16).astype(jnp.float32) * own_v
 
-    for i in (2, 3, 4):
-        prefill(i)
+    prefill(2, 3, 4)
 
     load_pages.wait()
     own_tab.wait()
@@ -244,8 +245,7 @@
             remote(k, z, lambda to: a_copy(to, chip).start())
     acc_recv[chip] = acc_send[chip]
     st_recv[chip] = st_send[chip]
-    for i in (5, 7):
-        prefill(i)
+    prefill(5, 7)
 
     for k, z in everywhere:
         remote(k, z, lambda of: t_copy(of, of).wait_recv())
@@ -279,8 +279,7 @@
         r_copy(u).start()
     part[0] = product(0).astype(jnp.bfloat16)
 
-    for i in (6,):
-        prefill(i)
+    prefill(6)
 
     sums = part[0].astype(jnp.float32)
     for u in range(1, n_t):

time: 39.4 us -> 38.8 us (0.985)
  Pallas kernels: 36.1 us -> 35.4 us
    pallas_call x1, Pallas kernels: 34.7 us -> 34 us  [body(): pl.pallas_call(functools.partial(kernel, chips_z), out_shape=(vm((samples...]
where the time goes in v2:
time: 38.8 us; the launch traced here: 38.1 us
  Pallas kernels  35.4 us (91%)
  between operations  2.74 us (7%)
    pallas_call x1, Pallas kernels, body(): pl.pallas_call(functools.partial(kernel, chips_z), out_shape=(vm((samples...  34 us
    pallas_call x1, Pallas kernels, body(): pl.pallas_call(store, out_shape=tuple((jax.ShapeDtypeStruct(out.shape, ou...  1.34 us

profile of v2, /device:TPU:1, one launch (start us, length us, event | category | flops | bytes accessed | tf_op | source)
XLA Modules:
  0.0 38.1 jit_solution(17500888406348733811)
XLA Ops:
  2.6 34.0 %shard_map.122 = (bf16[16,512]{1,0:T(8,128)(2,1)S(1)}, bf16[2048,512]{1,0:T(8,128)(2,1)S(1)}) custom-call(s32[1,1]{1,0:T(1,128)} %bitcast.4.plen_hbm, s32[1,1]{1,0:T(1,128)} %bitcast.5.scount_hbm, s32[1,1]{1,0:T(1,128)} %bitcast.6.slen_hbm, s32[1,24]{1,0:T(1,128)} %bitcast.7, bf16[16,512]{1,0:T(8,128)(2,1)} %dq_hbm.1, bf16[16,256]{1,0:T(8,128)(2,1)} %skv_hbm.1, ...), custom_call_target="tpu_custom_call" | custom-call | flops 6000000000 | bytes 12582912 | tf_op jit(solution)/shard_map/pallas_call | solution.py:324
  36.6 1.3 %shard_map.123 = (bf16[16,512]{1,0:T(8,128)(2,1)}, bf16[2048,512]{1,0:T(8,128)(2,1)}) custom-call(bf16[16,512]{1,0:T(8,128)(2,1)S(1)} %get-tuple-element.4.dec, bf16[2048,512]{1,0:T(8,128)(2,1)S(1)} %get-tuple-element.5.pre), custom_call_target="tpu_custom_call" | custom-call | tf_op jit(solution)/shard_map/pallas_call | solution.py:352
